TPU v7x, 32 devices: a whole 2x2x4 slice. The times are simulated.
32 devices in a mesh: frame: 4 (over y, x), crop: 4 (over z), dp: 2 (over core).
Axes of the slice: x: 2, y: 2, z: 4, core: 2. Of those that a mesh axis runs over, the one named last changes fastest.
Arguments:
- global_clips: bfloat16 [2, 16, 256, 1408], P('dp', 'frame', 'crop'), may hold values from -6 to 6
- frame_map: int32 [2, 16, 8], P('dp', 'crop'), may hold values from 0 to 15
- teacher_qkv: bfloat16 [1408, 4224], P(None, 'frame'), may hold values from -0.15625 to 0.15625
- teacher_out: bfloat16 [1408, 1408], P('frame'), may hold values from -0.15625 to 0.15625
- teacher_bottle: bfloat16 [1408, 256], replicated, may hold values from -0.15625 to 0.15625
- student_qkv: bfloat16 [1408, 4224], P(None, 'frame'), may hold values from -0.15625 to 0.15625
- student_out: bfloat16 [1408, 1408], P('frame'), may hold values from -0.15625 to 0.15625
- student_bottle: bfloat16 [1408, 256], replicated, may hold values from -0.15625 to 0.15625
- prototypes: bfloat16 [256, 8192], P(None, 'frame'), may hold values from -1.796875 to 1.796875
- center: float32 [8192], P('frame'), may hold values from -8.6 to -3.9
Outputs:
- grad_qkv: float32 [1408, 4224], P(('crop', 'dp'), 'frame')
- grad_out: float32 [1408, 1408], P('frame', ('crop', 'dp'))
- grad_bottle: float32 [1408, 256], P(('crop', 'dp'))
All inputs are finite; a program needn't handle non-finite values.
Results may differ from a plain program's by a relative error of at most 0.00035.
Values may be sent and summed in bfloat16 or wider, within the bound.
A program may use at most 128 MiB of HBM per device.

v0:
```python
import functools
import math

import jax
import jax.numpy as jnp
from jax import lax
from jax.experimental import pallas as pl
from jax.experimental.pallas import tpu as pltpu
from jax.sharding import PartitionSpec as P

HEAD = 88
HIGH = lax.Precision.HIGHEST
TAU_TEACH = 0.04
TAU_STUD = 0.1
SCALE = 1.0 / math.sqrt(HEAD)
NT = (((1,), (1,)), ((), ()))


def rounded(x):
    return x.astype(jnp.bfloat16).astype(jnp.float32)


def forward_kernel(
    maps, tokens, w_t, w_s, normed, sums, t_heads, s_heads, s_qkv, s_weights, s_cols, picked, t_qkv
):
    frames = tokens.shape[0]
    half = tokens.shape[1]
    heads = w_t.shape[0] // (3 * HEAD)
    pairs = frames // 2
    clips, steps = maps.shape

    def norm(f, _):
        x = tokens[f].astype(jnp.float32)
        middle = jnp.mean(x, axis=-1, keepdims=True)
        away = x - middle
        spread = jnp.mean(away * away, axis=-1, keepdims=True)
        normed[f] = (away * lax.rsqrt(spread + 1e-06)).astype(jnp.bfloat16)
        sums[pl.ds(f, 1)] = jnp.sum(x, axis=0, keepdims=True)
        return 0

    lax.fori_loop(0, frames, norm, 0)

    def project_t(a, _):
        x = jnp.concatenate([normed[2 * a], normed[2 * a + 1]], axis=0)
        t_qkv[a] = rounded(
            lax.dot_general(w_t[...], x, NT, preferred_element_type=jnp.float32)
        )
        return 0

    lax.fori_loop(0, pairs, project_t, 0)

    def attend_t(h, _):
        row = pl.multiple_of(h * (3 * HEAD), 8)
        keys = t_qkv[:, pl.ds(row + HEAD, HEAD), :]
        turned = pltpu.roll(keys, half, 2)
        same = jnp.zeros((pairs, 2 * half), jnp.float32)
        cross = jnp.zeros((pairs, 2 * half), jnp.float32)
        for a in range(pairs):
            query = t_qkv[a, pl.ds(row, HEAD), :]
            one = jnp.sum(query[None] * keys, axis=1) * SCALE
            two = jnp.sum(query[None] * turned, axis=1) * SCALE
            top = jnp.maximum(
                jnp.max(one, axis=0, keepdims=True), jnp.max(two, axis=0, keepdims=True)
            )
            one = jnp.exp(one - top)
            two = jnp.exp(two - top)
            total = jnp.sum(one, axis=0, keepdims=True) + jnp.sum(two, axis=0, keepdims=True)
            same = same + rounded(one / total)
            cross = cross + rounded(two / total)
        columns = same + pltpu.roll(cross, half, 1)
        out = jnp.zeros((HEAD, 2 * half), jnp.float32)
        for b in range(pairs):
            out = out + columns[b : b + 1, :] * t_qkv[b, pl.ds(row + 2 * HEAD, HEAD), :]
        t_heads[pl.ds(pl.multiple_of(h * HEAD, 8), HEAD), :] = out
        return 0

    lax.fori_loop(0, heads, attend_t, 0)

    for lp in range(clips // 2):

        def project_s(i, _):
            x = jnp.concatenate([normed[maps[2 * lp, i]], normed[maps[2 * lp + 1, i]]], axis=0)
            picked[lp, i] = x
            s_qkv[lp, i] = rounded(
                lax.dot_general(w_s[...], x, NT, preferred_element_type=jnp.float32)
            )
            return 0

        lax.fori_loop(0, steps, project_s, 0)

        def attend_s(h, _):
            row = pl.multiple_of(h * (3 * HEAD), 8)
            keys = s_qkv[lp, :, pl.ds(row + HEAD, HEAD), :]
            columns = jnp.zeros((steps, 2 * half), jnp.float32)
            for i in range(steps):
                query = s_qkv[lp, i, pl.ds(row, HEAD), :]
                one = jnp.sum(query[None] * keys, axis=1) * SCALE
                one = jnp.exp(one - jnp.max(one, axis=0, keepdims=True))
                one = one / jnp.sum(one, axis=0, keepdims=True)
                s_weights[lp, h, i] = one
                columns = columns + rounded(one)
            s_cols[lp, h] = columns
            out = jnp.zeros((HEAD, 2 * half), jnp.float32)
            for j in range(steps):
                out = out + columns[j : j + 1, :] * s_qkv[lp, j, pl.ds(row + 2 * HEAD, HEAD), :]
            s_heads[lp, pl.ds(pl.multiple_of(h * HEAD, 8), HEAD), :] = out
            return 0

        lax.fori_loop(0, heads, attend_s, 0)


def backward_kernel(grads, s_qkv, s_weights, s_cols, picked, g_qkv, d_rows, d_all, x_turned):
    pairs, steps, width, lanes = s_qkv.shape
    heads = width // (3 * HEAD)

    for lp in range(pairs):

        def attend(h, _):
            row = pl.multiple_of(h * (3 * HEAD), 8)
            grad = grads[lp, pl.ds(pl.multiple_of(h * HEAD, 8), HEAD), :]
            values = s_qkv[lp, :, pl.ds(row + 2 * HEAD, HEAD), :]
            d_weights = rounded(jnp.sum(values * grad[None], axis=1))
            d_scores = []
            for i in range(steps):
                weights = s_weights[lp, h, i]
                inner = jnp.sum(weights * d_weights, axis=0, keepdims=True)
                d_scores.append(weights * (d_weights - inner) * SCALE)
            for i in range(steps):
                d_query = jnp.zeros((HEAD, lanes), jnp.float32)
                for j in range(steps):
                    d_query = (
                        d_query
                        + d_scores[i][j : j + 1, :] * s_qkv[lp, j, pl.ds(row + HEAD, HEAD), :]
                    )
                d_rows[i, pl.ds(row, HEAD), :] = d_query
            columns = s_cols[lp, h]
            for j in range(steps):
                d_key = jnp.zeros((HEAD, lanes), jnp.float32)
                for i in range(steps):
                    d_key = (
                        d_key + d_scores[i][j : j + 1, :] * s_qkv[lp, i, pl.ds(row, HEAD), :]
                    )
                d_rows[j, pl.ds(row + HEAD, HEAD), :] = d_key
                d_rows[j, pl.ds(row + 2 * HEAD, HEAD), :] = columns[j : j + 1, :] * grad
            return 0

        lax.fori_loop(0, heads, attend, 0)
        for i in range(steps):
            at = (lp * steps + i) * lanes
            d_all[:, at : at + lanes] = d_rows[i].astype(jnp.bfloat16)
            x_turned[:, at : at + lanes] = picked[lp, i].T

    depth = x_turned.shape[0]
    block = depth // 4

    def multiply(n, _):
        at = pl.multiple_of(n * block, 16)
        g_qkv[pl.ds(at, block), :] = lax.dot_general(
            x_turned[pl.ds(at, block), :], d_all[...], NT, preferred_element_type=jnp.float32
        )
        return 0

    lax.fori_loop(0, 4, multiply, 0)


def vmem(count):
    return [pl.BlockSpec(memory_space=pltpu.VMEM)] * count


def forward(maps, tokens, w_t, w_s):
    frames, patches, width = tokens.shape
    columns = w_t.shape[0]
    heads = columns // (3 * HEAD)
    clips, steps = maps.shape
    lanes = 2 * patches
    f32, bf16 = jnp.float32, jnp.bfloat16
    shape = jax.ShapeDtypeStruct
    return pl.pallas_call(
        forward_kernel,
        out_shape=[
            shape((frames, patches, width), bf16),
            shape((frames, width), f32),
            shape((heads * HEAD, lanes), f32),
            shape((clips // 2, heads * HEAD, lanes), f32),
            shape((clips // 2, steps, columns, lanes), f32),
            shape((clips // 2, heads, steps, steps, lanes), f32),
            shape((clips // 2, heads, steps, lanes), f32),
            shape((clips // 2, steps, lanes, width), bf16),
        ],
        in_specs=[pl.BlockSpec(memory_space=pltpu.SMEM)] + vmem(3),
        out_specs=vmem(8),
        scratch_shapes=[pltpu.VMEM((frames // 2, columns, lanes), f32)],
        compiler_params=pltpu.CompilerParams(vmem_limit_bytes=56 * 1024 * 1024),
    )(maps, tokens, w_t, w_s)


def backward(grads, s_qkv, s_weights, s_cols, picked):
    pairs, steps, columns, lanes = s_qkv.shape
    width = picked.shape[-1]
    return pl.pallas_call(
        backward_kernel,
        out_shape=jax.ShapeDtypeStruct((width, columns), jnp.float32),
        in_specs=vmem(5),
        out_specs=vmem(1)[0],
        scratch_shapes=[
            pltpu.VMEM((steps, columns, lanes), jnp.float32),
            pltpu.VMEM((columns, pairs * steps * lanes), jnp.bfloat16),
            pltpu.VMEM((width, pairs * steps * lanes), jnp.bfloat16),
        ],
        compiler_params=pltpu.CompilerParams(vmem_limit_bytes=56 * 1024 * 1024),
    )(grads, s_qkv, s_weights, s_cols, picked)


def unit(vector):
    return vector * lax.rsqrt(jnp.sum(vector * vector, axis=-1, keepdims=True) + 1e-06)


def local(
    global_clips,
    frame_map,
    teacher_qkv,
    teacher_out,
    teacher_bottle,
    student_qkv,
    student_out,
    student_bottle,
    prototypes,
    center,
):
    f32 = jnp.float32
    tokens = global_clips[0]
    maps = frame_map[0]
    gathered = lax.all_gather(tokens, "frame", axis=0, tiled=True)
    frames_all, patches, width = gathered.shape
    clips, steps = maps.shape
    spread = lax.axis_size("crop") * lax.axis_size("dp")
    place = lax.axis_index("crop") * lax.axis_size("dp") + lax.axis_index("dp")
    teacher_count = frames_all * patches * lax.axis_size("crop")
    local_count = steps * patches

    _, sums, t_wide, s_wide, s_qkv, s_weights, s_cols, picked = forward(
        maps, gathered, teacher_qkv.T, student_qkv.T
    )
    rows = t_wide.shape[0]
    t_heads = jnp.sum(t_wide, axis=1)
    s_heads = (
        jnp.sum(s_wide.reshape(clips // 2, rows, 2, patches), axis=3)
        .transpose(0, 2, 1)
        .reshape(clips, rows)
    ) / local_count

    t_out32 = teacher_out.astype(f32)
    s_out32 = student_out.astype(f32)
    s_bottle32 = student_bottle.astype(f32)
    protos = prototypes.astype(f32)
    own = jnp.sum(tokens, axis=(0, 1), dtype=f32)
    t_partial = (own + jnp.dot(t_heads, t_out32, precision=HIGH)) / teacher_count
    t_z = jnp.dot(t_partial, teacher_bottle.astype(f32), precision=HIGH)
    s_partial = jnp.dot(s_heads, s_out32, precision=HIGH)
    picks = jnp.sum(
        (maps[:, :, None] == jnp.arange(frames_all, dtype=jnp.int32)[None, None, :]).astype(f32),
        axis=1,
    )
    local_mean = jnp.dot(picks, sums, precision=HIGH) / local_count

    packed = lax.psum(jnp.concatenate([s_partial.reshape(-1), t_z]), "frame")
    s_pooled = local_mean + packed[: clips * width].reshape(clips, width)
    unit_t = unit(lax.psum(packed[clips * width :], "crop"))
    s_z = jnp.dot(s_pooled, s_bottle32, precision=HIGH)
    inverse = lax.rsqrt(jnp.sum(s_z * s_z, axis=-1, keepdims=True) + 1e-06)
    unit_s = s_z * inverse

    units = jnp.concatenate([unit_s, unit_t[None]], axis=0)
    raw = jnp.dot(units, protos, precision=HIGH)
    logits = jnp.concatenate([raw[:clips] / TAU_STUD, (raw[clips:] - center) / TAU_TEACH], axis=0)
    top = jnp.max(logits, axis=-1, keepdims=True)
    weights = jnp.exp(logits - top)
    total = jnp.sum(weights, axis=-1, keepdims=True)
    expect = lax.dot_general(weights, protos, NT, precision=HIGH)
    shares = lax.all_gather(jnp.concatenate([expect, total, top], axis=1), "frame")
    bottle = expect.shape[1]
    tops = shares[:, :, bottle + 1 :]
    factor = jnp.exp(tops - jnp.max(tops, axis=0, keepdims=True))
    merged = jnp.sum(shares[:, :, : bottle + 1] * factor, axis=0)
    expect = merged[:, :bottle] / merged[:, bottle:]

    all_clips = clips * lax.axis_size("crop")
    d_unit = (expect[:clips] - expect[clips:]) / (all_clips * TAU_STUD)
    d_z = (d_unit - unit_s * jnp.sum(unit_s * d_unit, axis=-1, keepdims=True)) * inverse
    d_pooled = lax.dot_general(d_z, s_bottle32, NT, precision=HIGH)
    d_heads = lax.dot_general(d_pooled, s_out32, NT, precision=HIGH) / local_count

    wide = jnp.broadcast_to(
        d_heads.reshape(clips // 2, 2, rows).transpose(0, 2, 1)[..., None],
        (clips // 2, rows, 2, patches),
    ).reshape(clips // 2, rows, 2 * patches)
    g_qkv = backward(wide, s_qkv, s_weights, s_cols, picked)
    g_qkv = lax.psum_scatter(g_qkv, ("crop", "dp"), scatter_dimension=0, tiled=True)

    few = lax.all_gather(
        jnp.concatenate([s_heads, s_pooled, d_z], axis=1), ("crop", "dp"), axis=0, tiled=True
    )
    size = width // spread
    all_heads = few[:, :rows]
    all_pooled = lax.dynamic_slice_in_dim(few[:, rows : rows + width], place * size, size, axis=1)
    all_d_z = few[:, rows + width :]
    some_bottle = lax.dynamic_slice_in_dim(s_bottle32, place * size, size, axis=0)
    g_bottle = jnp.dot(all_pooled.T, all_d_z, precision=HIGH)
    d_some = lax.dot_general(all_d_z, some_bottle, NT, precision=HIGH)
    g_out = jnp.dot(all_heads.T, d_some, precision=HIGH)
    return g_qkv, g_out, g_bottle


def solution(mesh):
    return jax.shard_map(
        local,
        mesh=mesh,
        in_specs=(
            P("dp", "frame", "crop", None),
            P("dp", "crop", None),
            P(None, "frame"),
            P("frame", None),
            P(),
            P(None, "frame"),
            P("frame", None),
            P(),
            P(None, "frame"),
            P("frame"),
        ),
        out_specs=(P(("crop", "dp"), "frame"), P("frame", ("crop", "dp")), P(("crop", "dp"), None)),
        check_vma=False,
    )
```

profile of v0, /device:TPU:0, one launch (start us, length us, event | category | flops | bytes accessed | tf_op | source)
XLA Modules:
  0.0 246.2 jit_solution(3107460773359315446)
XLA Ops:
  7.2 0.7 all-gather.6.cloned.1.call-update
  8.0 0.8 convert_reduce_fusion.1
  8.7 1.2 convert_reduce_fusion
  10.0 44.4 %all-gather.6.cloned.1.call-done = bf16[1,16,64,1408]{3,2,0,1:T(8,128)(2,1)} async-done(((bf16[1,4,64,1408]{3,2,0,1:T(8,128)(2,1)}), bf16[1,16,64,1408]{3,2,0,1:T(8,128)(2,1)}) %all-gather.6.cloned.1.call-update) | async-done | bytes 2883600 | tf_op jit(solution)/shard_map/all_gather | solution.py:233
  54.4 42.4 %shard_map.121 = (bf16[16,64,1408]{2,1,0:T(8,128)(2,1)}, f32[16,1408]{1,0:T(8,128)}, f32[352,128]{1,0:T(8,128)}, f32[2,352,128]{2,1,0:T(8,128)}, f32[2,8,1056,12...) custom-call(s32[4,8]{1,0:T(4,128)} %bitcast.49, ...), custom_call_target="tpu_custom_call" | custom-call | tf_op jit(solution)/shard_map/pallas_call | solution.py:178
  96.8 1.1 reduce_sum.84
  98.0 1.7 convolution_reduce_fusion
  99.7 1.1 copy.26
  101.0 0.5 fusion.27
  101.5 1.5 fusion.28
  103.0 15.3 %psum.14 = f32[5888]{0:T(1024)S(1)} all-reduce(f32[5888]{0:T(1024)S(1)} %pad_maximum_fusion.1), channel_id=1, replica_groups=mesh['frame'=4,'crop'=4,'dp'=2] {'frame'}, use_global_device_ids=true, to_apply=%region_4.0 | all-reduce | flops 5888 | bytes 47104 | tf_op jit(solution)/shard_map/psum | solution.py:266
  118.4 11.7 %psum.15 = f32[256]{0:T(256)S(1)} all-reduce(f32[256]{0:T(256)S(1)} %slice.53), channel_id=1, replica_groups=mesh['frame'=4,'crop'=4,'dp'=2] {'crop'}, use_global_device_ids=true, to_apply=%region_6.0 | all-reduce | flops 256 | bytes 2048 | tf_op jit(solution)/shard_map/psum | solution.py:268
  130.0 0.6 multiply_reduce_fusion.2
  131.4 0.2 fusion
  131.6 0.5 multiply_reduce_fusion.1
  132.2 0.5 fusion.18
  132.8 0.1 fusion.4
  132.9 0.2 fusion.6
  133.1 0.9 fusion.7
  134.3 8.3 %all-gather.2 = f32[4,5,258]{2,1,0:T(8,128)S(1)} all-gather(f32[1,5,258]{2,1,0:T(8,128)S(1)} %maximum_bitcast_fusion), channel_id=3, replica_groups=mesh['frame'=4,'crop'=4,'dp'=2] {'frame'}, dimensions={0}, use_global_device_ids=true | all-gather | bytes 25800 | tf_op jit(solution)/shard_map/all_gather | solution.py:280
  142.6 0.2 slice_reduce_fusion
  142.8 0.2 exponential_reduce_fusion
  143.3 0.2 multiply_reduce_fusion
  143.5 0.7 fusion.29
  144.2 0.9 convolution_multiply_fusion.1
  145.2 0.9 copy.29.grads
  146.1 22.8 %shard_map.122 = f32[1408,1056]{1,0:T(8,128)} custom-call(f32[2,352,128]{2,1,0:T(8,128)} %copy.29.grads, f32[2,8,1056,128]{3,2,1,0:T(8,128)} %get-tuple-element.13.s_qkv, f32[2,4,8,8,128]{4,3,2,1,0:T(8,128)} %get-tuple-element.14.s_weights, f32[2,4,8,128]{3,2,1,0:T(8,128)} %get-tuple-element.15.s_cols, bf16[2,8,128,1408]{3,2,1,0:T(8,128)(2,1)} %get-tuple-element.16.picked), custom_call_target="tpu_custom_call" | custom-call | tf_op jit(solution)/shard_map/pallas_call | solution.py:200
  169.0 15.2 %all-gather.3 = f32[8,4,2016]{2,1,0:T(4,128)S(1)} all-gather(f32[1,4,2016]{2,1,0:T(4,128)S(1)} %bitcast.43), channel_id=1, replica_groups=mesh['frame'=4,'crop'=4,'dp'=2] {'crop','dp'}, dimensions={0}, use_global_device_ids=true | all-gather | bytes 290304 | tf_op jit(solution)/shard_map/all_gather | solution.py:300
  184.5 0.3 fusion.1
  184.7 1.1 fusion.12
  185.8 1.1 fusion.9
  186.9 52.4 %reduce-scatter.2.cloned.1.call-done = f32[176,1056]{1,0:T(8,128)} async-done(((f32[1408,1056]{1,0:T(8,128)}), f32[176,1056]{1,0:T(8,128)}) %reduce-scatter.2.cloned.1.call-update) | async-done | bytes 743440 | tf_op jit(solution)/shard_map/reduce_scatter | solution.py:298
  (41 shorter events, 1.4 us)
Async XLA Ops:
  7.2 125.0 %copy-start = (bf16[256,2048]{1,0:T(8,128)(2,1)S(1)}, bf16[256,2048]{1,0:T(8,128)(2,1)}, u32[]{:S(2)}) copy-start(bf16[256,2048]{1,0:T(8,128)(2,1)} %param.18) | copy-start | bytes 3145732
  7.2 47.2 %all-gather.6.cloned.1.call-start = ((), (), s32[]{:S(2)}) async-start(), calls=%async_computation.2 | async-start | bytes 3604480 | tf_op jit(solution)/shard_map/all_gather | solution.py:233
  7.9 231.4 %reduce-scatter.2.cloned.1.call-start = ((), (), s32[]{:S(2)}) async-start(), calls=%async_computation.1 | async-start | bytes 7299072 | tf_op jit(solution)/shard_map/reduce_scatter | solution.py:298
  54.4 46.6 %copy-start.1 = (bf16[352,1408]{1,0:T(8,128)(2,1)S(1)}, bf16[352,1408]{1,0:T(8,128)(2,1)}, u32[]{:S(2)}) copy-start(bf16[352,1408]{1,0:T(8,128)(2,1)} %param.16) | copy-start | bytes 2973700
  96.8 34.5 %copy-start.3 = (f32[16,1408]{1,0:T(8,128)S(1)}, f32[16,1408]{1,0:T(8,128)}, u32[]{:S(2)}) copy-start(f32[16,1408]{1,0:T(8,128)} %get-tuple-element.10) | copy-start | bytes 270340
  96.8 34.7 %copy-start.2 = (bf16[1408,256]{1,0:T(8,128)(2,1)S(1)}, bf16[1408,256]{1,0:T(8,128)(2,1)}, u32[]{:S(2)}) copy-start(bf16[1408,256]{1,0:T(8,128)(2,1)} %param.17) | copy-start | bytes 2162692
  98.0 34.7 %copy-start.4 = (f32[2048]{0:T(1024)S(1)}, f32[2048]{0:T(1024)}, u32[]{:S(2)}) copy-start(f32[2048]{0:T(1024)} %param.19) | copy-start | bytes 24580
Sparse Core Ops, SparseCore 0:
  9.9 44.4 all-gather.5
  169.0 70.2 reduce-scatter.1
where the time goes:
time: 247 us; the launch traced here: 246 us
  waiting for transfers between devices  97.6 us (40%)
  Pallas kernels  65.2 us (26%)
  blocking collectives  50.5 us (20%)
  between operations  14.9 us (6%)
  matrix products  9.92 us (4%)
  other arithmetic  5.11 us (2%)
  local copies, waits for them, and re-layouts  2.83 us (1%)
    reduce_scatter x1, waiting for transfers between devices, local(): lax.psum_scatter(g_qkv, ('crop', 'dp'), scatter_dimension=0, tiled=True)  52.4 us
    all_gather x1, waiting for transfers between devices, local(): gathered = lax.all_gather(tokens, 'frame', axis=0, tiled=True)  44.4 us
    pallas_call x1, Pallas kernels, forward(): pl.pallas_call(forward_kernel, out_shape=[shape((frames, patches, width),...  42.4 us
    pallas_call x1, Pallas kernels, backward(): pl.pallas_call(backward_kernel, out_shape=jax.ShapeDtypeStruct((width, co...  22.8 us
    psum x1, blocking collectives, local(): packed = lax.psum(jnp.concatenate([s_partial.reshape(-1), t_z]), 'frame')  15.3 us
    all_gather x1, blocking collectives, local(): lax.all_gather(jnp.concatenate([s_heads, s_pooled, d_z], axis=1), ('crop'...  15.2 us
    psum x1, blocking collectives, local(): unit_t = unit(lax.psum(packed[clips * width:], 'crop'))  11.7 us
    all_gather x1, blocking collectives, local(): lax.all_gather(jnp.concatenate([expect, total, top], axis=1), 'frame')  8.34 us
  transfers between devices with their start and end apart: 2, of which 2 were waited for; matrix products, arithmetic and copies ran while one was open for 2% of the time, Pallas kernels for 0%

commit v1 on v0

--- a/solution.py
+++ b/solution.py
@@ -20,34 +20,176 @@
     return x.astype(jnp.bfloat16).astype(jnp.float32)
 
 
-def forward_kernel(
-    maps, tokens, w_t, w_s, normed, sums, t_heads, s_heads, s_qkv, s_weights, s_cols, picked, t_qkv
+MESH = pl.DeviceIdType.MESH
+
+
+def greet(peers):
+    barrier = pltpu.get_barrier_semaphore()
+    for peer in peers:
+        pl.semaphore_signal(barrier, inc=1, device_id=peer, device_id_type=MESH)
+    pl.semaphore_wait(barrier, len(peers))
+
+
+def gather_kernel(
+    count, tokens, w_t, w_s, normed, sums, t_qkv, s_frames, held, send_sems, recv_sems
 ):
-    frames = tokens.shape[0]
+    me = lax.axis_index("frame")
+    each = tokens.shape[0]
     half = tokens.shape[1]
-    heads = w_t.shape[0] // (3 * HEAD)
-    pairs = frames // 2
-    clips, steps = maps.shape
-
-    def norm(f, _):
-        x = tokens[f].astype(jnp.float32)
+    peers = [{"frame": lax.rem(me + s, count)} for s in range(1, count)]
+    greet(peers)
+    copies = []
+    for s, peer in enumerate(peers):
+        copy = pltpu.make_async_remote_copy(
+            src_ref=tokens,
+            dst_ref=held.at[me],
+            send_sem=send_sems.at[s],
+            recv_sem=recv_sems.at[s],
+            device_id=peer,
+            device_id_type=MESH,
+        )
+        copy.start()
+        copies.append(copy)
+
+    def norm(x, f):
+        x = x.astype(jnp.float32)
         middle = jnp.mean(x, axis=-1, keepdims=True)
         away = x - middle
         spread = jnp.mean(away * away, axis=-1, keepdims=True)
-        normed[f] = (away * lax.rsqrt(spread + 1e-06)).astype(jnp.bfloat16)
-        sums[pl.ds(f, 1)] = jnp.sum(x, axis=0, keepdims=True)
+        out = (away * lax.rsqrt(spread + 1e-06)).astype(jnp.bfloat16)
+        normed[f] = out
+        sums[f] = jnp.sum(x, axis=0, keepdims=True)
+
+    def project(pair):
+        f = 2 * pair
+        x = jnp.concatenate([normed[f], normed[f + 1]], axis=0)
+        t_qkv[pair] = lax.dot_general(
+            w_t[...], x, NT, preferred_element_type=jnp.float32
+        ).astype(jnp.bfloat16)
+        y = lax.dot_general(w_s[...], x, NT, preferred_element_type=jnp.float32)
+        turned = pltpu.roll(y, half, 1)
+        low = lax.broadcasted_iota(jnp.int32, y.shape, 1) < half
+        s_frames[f] = jnp.where(low, y, turned).astype(jnp.bfloat16)
+        s_frames[f + 1] = jnp.where(low, turned, y).astype(jnp.bfloat16)
+
+    paired = each % 2 == 0
+
+    def work(load, source):
+        def one(k, _):
+            norm(load(k), source * each + k)
+            return 0
+
+        def two(k, _):
+            project(source * (each // 2) + k)
+            return 0
+
+        lax.fori_loop(0, each, one, 0)
+        if paired:
+            lax.fori_loop(0, each // 2, two, 0)
+
+    work(lambda k: tokens[k], me)
+    for s in range(1, count):
+        copies[s - 1].wait_recv()
+        source = lax.rem(me + count - s, count)
+        work(lambda k, source=source: held[source, k], source)
+    if not paired:
+
+        def late(k, _):
+            project(k)
+            return 0
+
+        lax.fori_loop(0, t_qkv.shape[0], late, 0)
+    for copy in copies:
+        copy.wait_send()
+
+
+def share_sum_kernel(
+    frames, crops, part, small, part_sum, small_sum, held, held_small, sends, recvs, sends_b, recvs_b
+):
+    me = lax.axis_index("frame")
+    layer = lax.axis_index("crop")
+    mine = layer * frames + me
+    shifts = [(c, s) for c in range(crops) for s in range(frames) if c + s > 0]
+    peers = [
+        {"frame": lax.rem(me + s, frames), "crop": lax.rem(layer + c, crops)} for c, s in shifts
+    ]
+    greet(peers)
+    copies = []
+    for n, ((c, s), peer) in enumerate(zip(shifts, peers)):
+        if c == 0:
+            copies.append(
+                pltpu.make_async_remote_copy(
+                    src_ref=part,
+                    dst_ref=held.at[me],
+                    send_sem=sends.at[s - 1],
+                    recv_sem=recvs.at[s - 1],
+                    device_id=peer,
+                    device_id_type=MESH,
+                )
+            )
+            copies[-1].start()
+    for n, peer in enumerate(peers):
+        copies.append(
+            pltpu.make_async_remote_copy(
+                src_ref=small,
+                dst_ref=held_small.at[mine],
+                send_sem=sends_b.at[n],
+                recv_sem=recvs_b.at[n],
+                device_id=peer,
+                device_id_type=MESH,
+            )
+        )
+        copies[-1].start()
+    held[me] = part[...]
+    held_small[mine] = small[...]
+    for copy in copies:
+        copy.wait()
+    total = held[0]
+    for f in range(1, frames):
+        total = total + held[f]
+    part_sum[...] = total
+    total = held_small[0]
+    for f in range(1, frames * crops):
+        total = total + held_small[f]
+    small_sum[...] = total
+
+
+def share_kernel(frames, part, out, held, sends, recvs):
+    me = lax.axis_index("frame")
+    peers = [{"frame": lax.rem(me + s, frames)} for s in range(1, frames)]
+    greet(peers)
+    copies = []
+    for n, peer in enumerate(peers):
+        copies.append(
+            pltpu.make_async_remote_copy(
+                src_ref=part,
+                dst_ref=held.at[me],
+                send_sem=sends.at[n],
+                recv_sem=recvs.at[n],
+                device_id=peer,
+                device_id_type=MESH,
+            )
+        )
+        copies[-1].start()
+    held[me] = part[...]
+    for copy in copies:
+        copy.wait()
+    out[...] = held[...]
+
+
+def forward_kernel(
+    maps, t_half, s_frames, t_heads, s_heads, s_qkv, s_weights, s_cols, t_qkv
+):
+    pairs, columns_all, lanes = t_half.shape
+    half = lanes // 2
+    heads = columns_all // (3 * HEAD)
+    clips, steps = maps.shape
+
+    def widen(a, _):
+        t_qkv[a] = t_half[a].astype(jnp.float32)
         return 0
 
-    lax.fori_loop(0, frames, norm, 0)
-
-    def project_t(a, _):
-        x = jnp.concatenate([normed[2 * a], normed[2 * a + 1]], axis=0)
-        t_qkv[a] = rounded(
-            lax.dot_general(w_t[...], x, NT, preferred_element_type=jnp.float32)
-        )
-        return 0
-
-    lax.fori_loop(0, pairs, project_t, 0)
+    lax.fori_loop(0, pairs, widen, 0)
 
     def attend_t(h, _):
         row = pl.multiple_of(h * (3 * HEAD), 8)
@@ -79,10 +221,11 @@
     for lp in range(clips // 2):
 
         def project_s(i, _):
-            x = jnp.concatenate([normed[maps[2 * lp, i]], normed[maps[2 * lp + 1, i]]], axis=0)
-            picked[lp, i] = x
-            s_qkv[lp, i] = rounded(
-                lax.dot_general(w_s[...], x, NT, preferred_element_type=jnp.float32)
+            low = lax.broadcasted_iota(jnp.int32, (columns_all, lanes), 1) < half
+            s_qkv[lp, i] = jnp.where(
+                low,
+                s_frames[maps[2 * lp, i]].astype(jnp.float32),
+                s_frames[maps[2 * lp + 1, i]].astype(jnp.float32),
             )
             return 0
 
@@ -109,14 +252,17 @@
         lax.fori_loop(0, heads, attend_s, 0)
 
 
-def backward_kernel(grads, s_qkv, s_weights, s_cols, picked, g_qkv, d_rows, d_all, x_turned):
-    pairs, steps, width, lanes = s_qkv.shape
-    heads = width // (3 * HEAD)
+def backward_kernel(
+    first, heads, maps, grads, s_qkv, s_weights, s_cols, normed, g_qkv, d_rows, d_all, x_turned
+):
+    pairs, steps, _, lanes = s_qkv.shape
 
     for lp in range(pairs):
 
-        def attend(h, _):
+        def attend(n, _):
+            h = first + n
             row = pl.multiple_of(h * (3 * HEAD), 8)
+            own = pl.multiple_of(n * (3 * HEAD), 8)
             grad = grads[lp, pl.ds(pl.multiple_of(h * HEAD, 8), HEAD), :]
             values = s_qkv[lp, :, pl.ds(row + 2 * HEAD, HEAD), :]
             d_weights = rounded(jnp.sum(values * grad[None], axis=1))
@@ -132,7 +278,7 @@
                         d_query
                         + d_scores[i][j : j + 1, :] * s_qkv[lp, j, pl.ds(row + HEAD, HEAD), :]
                     )
-                d_rows[i, pl.ds(row, HEAD), :] = d_query
+                d_rows[i, pl.ds(own, HEAD), :] = d_query
             columns = s_cols[lp, h]
             for j in range(steps):
                 d_key = jnp.zeros((HEAD, lanes), jnp.float32)
@@ -140,15 +286,16 @@
                     d_key = (
                         d_key + d_scores[i][j : j + 1, :] * s_qkv[lp, i, pl.ds(row, HEAD), :]
                     )
-                d_rows[j, pl.ds(row + HEAD, HEAD), :] = d_key
-                d_rows[j, pl.ds(row + 2 * HEAD, HEAD), :] = columns[j : j + 1, :] * grad
+                d_rows[j, pl.ds(own + HEAD, HEAD), :] = d_key
+                d_rows[j, pl.ds(own + 2 * HEAD, HEAD), :] = columns[j : j + 1, :] * grad
             return 0
 
         lax.fori_loop(0, heads, attend, 0)
         for i in range(steps):
             at = (lp * steps + i) * lanes
             d_all[:, at : at + lanes] = d_rows[i].astype(jnp.bfloat16)
-            x_turned[:, at : at + lanes] = picked[lp, i].T
+            x = jnp.concatenate([normed[maps[2 * lp, i]], normed[maps[2 * lp + 1, i]]], axis=0)
+            x_turned[:, at : at + lanes] = x.T
 
     depth = x_turned.shape[0]
     block = depth // 4
@@ -167,48 +314,111 @@
     return [pl.BlockSpec(memory_space=pltpu.VMEM)] * count
 
 
-def forward(maps, tokens, w_t, w_s):
-    frames, patches, width = tokens.shape
+def limits(**more):
+    return pltpu.CompilerParams(vmem_limit_bytes=56 * 1024 * 1024, **more)
+
+
+def gather(tokens, w_t, w_s):
+    count = lax.axis_size("frame")
+    each, patches, width = tokens.shape
     columns = w_t.shape[0]
+    frames, lanes = count * each, 2 * patches
+    f32, bf16 = jnp.float32, jnp.bfloat16
+    shape = jax.ShapeDtypeStruct
+    return pl.pallas_call(
+        functools.partial(gather_kernel, count),
+        out_shape=[
+            shape((frames, patches, width), bf16),
+            shape((frames, 1, width), f32),
+            shape((frames // 2, columns, lanes), bf16),
+            shape((frames, columns, lanes), bf16),
+        ],
+        in_specs=vmem(3),
+        out_specs=vmem(4),
+        scratch_shapes=[
+            pltpu.VMEM((count, each, patches, width), bf16),
+            pltpu.SemaphoreType.DMA((count - 1,)),
+            pltpu.SemaphoreType.DMA((count - 1,)),
+        ],
+        compiler_params=limits(collective_id=0, has_side_effects=True),
+    )(tokens, w_t, w_s)
+
+
+def share_sum(part, small):
+    frames, crops = lax.axis_size("frame"), lax.axis_size("crop")
+    shape = jax.ShapeDtypeStruct
+    dma = pltpu.SemaphoreType.DMA
+    return pl.pallas_call(
+        functools.partial(share_sum_kernel, frames, crops),
+        out_shape=[shape(part.shape, part.dtype), shape(small.shape, small.dtype)],
+        in_specs=vmem(2),
+        out_specs=vmem(2),
+        scratch_shapes=[
+            pltpu.VMEM((frames,) + part.shape, part.dtype),
+            pltpu.VMEM((frames * crops,) + small.shape, small.dtype),
+            dma((frames - 1,)),
+            dma((frames - 1,)),
+            dma((frames * crops - 1,)),
+            dma((frames * crops - 1,)),
+        ],
+        compiler_params=pltpu.CompilerParams(collective_id=1, has_side_effects=True),
+    )(part, small)
+
+
+def share(part):
+    frames = lax.axis_size("frame")
+    return pl.pallas_call(
+        functools.partial(share_kernel, frames),
+        out_shape=jax.ShapeDtypeStruct((frames,) + part.shape, part.dtype),
+        in_specs=vmem(1),
+        out_specs=vmem(1)[0],
+        scratch_shapes=[
+            pltpu.VMEM((frames,) + part.shape, part.dtype),
+            pltpu.SemaphoreType.DMA((frames - 1,)),
+            pltpu.SemaphoreType.DMA((frames - 1,)),
+        ],
+        compiler_params=pltpu.CompilerParams(collective_id=2, has_side_effects=True),
+    )(part)
+
+
+def forward(maps, t_half, s_frames):
+    pairs, columns, lanes = t_half.shape
     heads = columns // (3 * HEAD)
     clips, steps = maps.shape
-    lanes = 2 * patches
-    f32, bf16 = jnp.float32, jnp.bfloat16
+    f32 = jnp.float32
     shape = jax.ShapeDtypeStruct
     return pl.pallas_call(
         forward_kernel,
         out_shape=[
-            shape((frames, patches, width), bf16),
-            shape((frames, width), f32),
             shape((heads * HEAD, lanes), f32),
             shape((clips // 2, heads * HEAD, lanes), f32),
             shape((clips // 2, steps, columns, lanes), f32),
             shape((clips // 2, heads, steps, steps, lanes), f32),
             shape((clips // 2, heads, steps, lanes), f32),
-            shape((clips // 2, steps, lanes, width), bf16),
         ],
-        in_specs=[pl.BlockSpec(memory_space=pltpu.SMEM)] + vmem(3),
-        out_specs=vmem(8),
-        scratch_shapes=[pltpu.VMEM((frames // 2, columns, lanes), f32)],
-        compiler_params=pltpu.CompilerParams(vmem_limit_bytes=56 * 1024 * 1024),
-    )(maps, tokens, w_t, w_s)
-
-
-def backward(grads, s_qkv, s_weights, s_cols, picked):
-    pairs, steps, columns, lanes = s_qkv.shape
-    width = picked.shape[-1]
+        in_specs=[pl.BlockSpec(memory_space=pltpu.SMEM)] + vmem(2),
+        out_specs=vmem(5),
+        scratch_shapes=[pltpu.VMEM((pairs, columns, lanes), f32)],
+        compiler_params=limits(),
+    )(maps, t_half, s_frames)
+
+
+def backward(first, heads, maps, grads, s_qkv, s_weights, s_cols, normed):
+    pairs, steps, _, lanes = s_qkv.shape
+    columns = heads * 3 * HEAD
+    width = normed.shape[-1]
     return pl.pallas_call(
-        backward_kernel,
+        functools.partial(backward_kernel, first, heads),
         out_shape=jax.ShapeDtypeStruct((width, columns), jnp.float32),
-        in_specs=vmem(5),
+        in_specs=[pl.BlockSpec(memory_space=pltpu.SMEM)] + vmem(5),
         out_specs=vmem(1)[0],
         scratch_shapes=[
             pltpu.VMEM((steps, columns, lanes), jnp.float32),
             pltpu.VMEM((columns, pairs * steps * lanes), jnp.bfloat16),
             pltpu.VMEM((width, pairs * steps * lanes), jnp.bfloat16),
         ],
-        compiler_params=pltpu.CompilerParams(vmem_limit_bytes=56 * 1024 * 1024),
-    )(grads, s_qkv, s_weights, s_cols, picked)
+        compiler_params=limits(),
+    )(maps, grads, s_qkv, s_weights, s_cols, normed)
 
 
 def unit(vector):
@@ -230,17 +440,16 @@
     f32 = jnp.float32
     tokens = global_clips[0]
     maps = frame_map[0]
-    gathered = lax.all_gather(tokens, "frame", axis=0, tiled=True)
-    frames_all, patches, width = gathered.shape
+    normed, sums, t_half, s_frames = gather(tokens, teacher_qkv.T, student_qkv.T)
+    frames_all, patches, width = normed.shape
+    sums = sums[:, 0]
     clips, steps = maps.shape
     spread = lax.axis_size("crop") * lax.axis_size("dp")
     place = lax.axis_index("crop") * lax.axis_size("dp") + lax.axis_index("dp")
     teacher_count = frames_all * patches * lax.axis_size("crop")
     local_count = steps * patches
 
-    _, sums, t_wide, s_wide, s_qkv, s_weights, s_cols, picked = forward(
-        maps, gathered, teacher_qkv.T, student_qkv.T
-    )
+    t_wide, s_wide, s_qkv, s_weights, s_cols = forward(maps, t_half, s_frames)
     rows = t_wide.shape[0]
     t_heads = jnp.sum(t_wide, axis=1)
     s_heads = (
@@ -263,9 +472,12 @@
     )
     local_mean = jnp.dot(picks, sums, precision=HIGH) / local_count
 
-    packed = lax.psum(jnp.concatenate([s_partial.reshape(-1), t_z]), "frame")
-    s_pooled = local_mean + packed[: clips * width].reshape(clips, width)
-    unit_t = unit(lax.psum(packed[clips * width :], "crop"))
+    bottle = t_z.shape[0]
+    summed, t_sum = share_sum(
+        s_partial.reshape(-1, 128), jnp.pad(t_z.reshape(-1, 128), ((0, 8 - bottle // 128), (0, 0)))
+    )
+    s_pooled = local_mean + summed.reshape(clips, width)
+    unit_t = unit(t_sum[: bottle // 128].reshape(-1))
     s_z = jnp.dot(s_pooled, s_bottle32, precision=HIGH)
     inverse = lax.rsqrt(jnp.sum(s_z * s_z, axis=-1, keepdims=True) + 1e-06)
     unit_s = s_z * inverse
@@ -277,8 +489,11 @@
     weights = jnp.exp(logits - top)
     total = jnp.sum(weights, axis=-1, keepdims=True)
     expect = lax.dot_general(weights, protos, NT, precision=HIGH)
-    shares = lax.all_gather(jnp.concatenate([expect, total, top], axis=1), "frame")
-    bottle = expect.shape[1]
+    shares = share(
+        jnp.pad(
+            jnp.concatenate([expect, total, top], axis=1), ((0, 7 - clips), (0, 126))
+        )
+    )[:, : clips + 1, : bottle + 2]
     tops = shares[:, :, bottle + 1 :]
     factor = jnp.exp(tops - jnp.max(tops, axis=0, keepdims=True))
     merged = jnp.sum(shares[:, :, : bottle + 1] * factor, axis=0)
@@ -294,8 +509,19 @@
         d_heads.reshape(clips // 2, 2, rows).transpose(0, 2, 1)[..., None],
         (clips // 2, rows, 2, patches),
     ).reshape(clips // 2, rows, 2 * patches)
-    g_qkv = backward(wide, s_qkv, s_weights, s_cols, picked)
-    g_qkv = lax.psum_scatter(g_qkv, ("crop", "dp"), scatter_dimension=0, tiled=True)
+    heads = rows // HEAD
+    first = heads // 2
+    shares_g = [
+        lax.psum_scatter(
+            backward(at, many, maps, wide, s_qkv, s_weights, s_cols, normed),
+            ("crop", "dp"),
+            scatter_dimension=0,
+            tiled=True,
+        )
+        for at, many in ((0, first), (first, heads - first))
+        if many
+    ]
+    g_qkv = jnp.concatenate(shares_g, axis=1)
 
     few = lax.all_gather(
         jnp.concatenate([s_heads, s_pooled, d_z], axis=1), ("crop", "dp"), axis=0, tiled=True

time: 247 us -> 228 us (0.923)
  Pallas kernels: 65.2 us -> 113 us
  waiting for transfers between devices: 97.6 us -> 57.5 us
  blocking collectives: 50.5 us -> 15.7 us
  other arithmetic: 5.11 us -> 11.5 us
    pallas_call x2 -> x6, Pallas kernels: 65.2 us -> 113 us  [the longest x1 51.3 us: gather(): pl.pallas_call(functools.partial(gather_kernel, count), out_shape=[shape(...]
    all_gather x1 -> x0, waiting for transfers between devices: 44.4 us -> none  [local(): gathered = lax.all_gather(tokens, 'frame', axis=0, tiled=True)]
    psum x2 -> x0, blocking collectives: 27 us -> none  [the longest x1 15.3 us: local(): packed = lax.psum(jnp.concatenate([s_partial.reshape(-1), t_z]), 'frame')]
    all_gather x1 -> x0, blocking collectives: 8.34 us -> none  [local(): lax.all_gather(jnp.concatenate([expect, total, top], axis=1), 'frame')]
    reduce_scatter x1 -> x2, waiting for transfers between devices: 52.4 us -> 57.4 us  [local(): lax.psum_scatter(backward(at, many, maps, wide, s_qkv, s_weights, s_cols,...]
    concatenate x1 -> x2, other arithmetic: 0.01 us -> 2.91 us  [the longest x1 2.22 us: local(): g_qkv = jnp.concatenate(shares_g, axis=1)]
  transfers between devices with their start and end apart: 2 -> 2, of which waited for: 2 -> 2; matrix products, arithmetic and copies ran while one was open for 2% -> 1% of each run, Pallas kernels for 0% -> 7%
where the time goes in v1:
time: 228 us; the launch traced here: 227 us
  Pallas kernels  113 us (50%)
  waiting for transfers between devices  57.5 us (25%)
  blocking collectives  15.7 us (7%)
  between operations  14.9 us (7%)
  other arithmetic  11.5 us (5%)
  matrix products  9.9 us (4%)
  local copies, waits for them, and re-layouts  4.86 us (2%)
    reduce_scatter x2, waiting for transfers between devices, local(): lax.psum_scatter(backward(at, many, maps, wide, s_qkv, s_weights, s_cols,...  57.4 us
    pallas_call x1, Pallas kernels, gather(): pl.pallas_call(functools.partial(gather_kernel, count), out_shape=[shape(...  51.3 us
    pallas_call x2, Pallas kernels, backward(): pl.pallas_call(functools.partial(backward_kernel, first, heads), out_shap...  31.5 us
    all_gather x1, blocking collectives, local(): lax.all_gather(jnp.concatenate([s_heads, s_pooled, d_z], axis=1), ('crop'...  15.7 us
    pallas_call x1, Pallas kernels, forward(): pl.pallas_call(forward_kernel, out_shape=[shape((heads * HEAD, lanes), f3...  14 us
    pallas_call x1, Pallas kernels, share_sum(): pl.pallas_call(functools.partial(share_sum_kernel, frames, crops), out_sh...  10.1 us
    pallas_call x1, Pallas kernels, share(): pl.pallas_call(functools.partial(share_kernel, frames), out_shape=jax.Sha...  6.06 us
  transfers between devices with their start and end apart: 2, of which 2 were waited for; matrix products, arithmetic and copies ran while one was open for 1% of the time, Pallas kernels for 7%

profile of v1, /device:TPU:0, one launch (start us, length us, event | category | flops | bytes accessed | tf_op | source)
XLA Modules:
  0.0 227.4 jit_solution(9893682487485491528)
XLA Ops:
  7.2 1.3 convert_reduce_fusion
  8.5 0.8 convert_reduce_fusion.1
  9.3 51.3 %shard_map.121 = (bf16[16,64,1408]{2,1,0:T(8,128)(2,1)}, f32[16,1,1408]{2,1,0:T(1,128)}, bf16[8,1056,128]{2,1,0:T(8,128)(2,1)}, bf16[16,1056,128]{2,1,0:T(8,128)(2,1)}) custom-call(bf16[4,64,1408]{2,1,0:T(8,128)(2,1)} %bitcast.41, bf16[1056,1408]{1,0:T(8,128)(2,1)} %bitcast.39, bf16[1056,1408]{1,0:T(8,128)(2,1)} %bitcast.40), custom_call_target="tpu_custom_call" | custom-call | tf_op jit(solution)/shard_map/pallas_call | solution.py:328
  60.6 14.0 %shard_map.122 = (f32[352,128]{1,0:T(8,128)}, f32[2,352,128]{2,1,0:T(8,128)}, f32[2,8,1056,128]{3,2,1,0:T(8,128)}, f32[2,4,8,8,128]{4,3,2,1,0:T(8,128)}, f32[2,4,8,128]{3,2,1,0:T(8,128)}) custom-call(s32[4,8]{1,0:T(4,128)} %bitcast.45, bf16[8,1056,128]{2,1,0:T(8,128)(2,1)} %get-tuple-element.15.t_half, bf16[16,1056,128]{2,1,0:T(8,128)(2,1)} %get-tuple-element.16.s_frames), custom_call_target="tpu_custom_call" | custom-call | tf_op jit(solution)/shard_map/pallas_call | solution.py:390
  74.6 1.2 copy.26
  76.5 0.6 reshape.60.part
  77.1 1.1 reduce_sum.84
  78.2 1.7 convolution_reduce_fusion
  79.9 1.5 fusion.29
  81.4 0.6 pad.8.small
  82.0 10.1 %shard_map.123 = (f32[44,128]{1,0:T(8,128)}, f32[8,128]{1,0:T(8,128)}) custom-call(f32[44,128]{1,0:T(8,128)} %reshape.60.part, f32[8,128]{1,0:T(8,128)} %pad.8.small), custom_call_target="tpu_custom_call" | custom-call | tf_op jit(solution)/shard_map/pallas_call | solution.py:351
  92.1 0.8 reshape.62
  93.6 1.3 multiply_reduce_fusion.3
  95.6 0.7 slice_multiply_fusion.1
  96.3 0.5 fusion.19
  97.0 0.9 fusion.9
  98.3 0.7 select_maximum_fusion.part
  99.0 6.1 %shard_map.124 = f32[4,8,384]{2,1,0:T(8,128)} custom-call(f32[8,384]{1,0:T(8,128)} %select_maximum_fusion.part), custom_call_target="tpu_custom_call" | custom-call | tf_op jit(solution)/shard_map/pallas_call | solution.py:370
  105.1 0.9 slice_reduce_fusion
  106.0 0.9 exponential_reduce_fusion
  106.9 0.9 multiply_reduce_fusion
  108.2 0.7 fusion.30
  108.9 0.9 convolution_multiply_fusion.1
  109.9 0.9 copy.29.grads
  110.8 15.8 %shard_map.125 = f32[1408,528]{1,0:T(8,128)} custom-call(s32[4,8]{1,0:T(4,128)} %bitcast.46, f32[2,352,128]{2,1,0:T(8,128)} %copy.29.grads, f32[2,8,1056,128]{3,2,1,0:T(8,128)} %get-tuple-element.21.s_qkv, f32[2,4,8,8,128]{4,3,2,1,0:T(8,128)} %get-tuple-element.22.s_weights, f32[2,4,8,128]{3,2,1,0:T(8,128)} %get-tuple-element.23.s_cols, ...), custom_call_target="tpu_custom_call" | custom-call | tf_op jit(solution)/shard_map/pallas_call | solution.py:410
  126.7 15.7 %shard_map.126 = f32[1408,528]{1,0:T(8,128)} custom-call(s32[4,8]{1,0:T(4,128)} %bitcast.47, f32[2,352,128]{2,1,0:T(8,128)} %copy.29.grads, f32[2,8,1056,128]{3,2,1,0:T(8,128)} %get-tuple-element.21.s_qkv, f32[2,4,8,8,128]{4,3,2,1,0:T(8,128)} %get-tuple-element.22.s_weights, f32[2,4,8,128]{3,2,1,0:T(8,128)} %get-tuple-element.23.s_cols, ...), custom_call_target="tpu_custom_call" | custom-call | tf_op jit(solution)/shard_map/pallas_call | solution.py:410
  142.5 15.7 %all-gather = f32[8,4,2016]{2,1,0:T(4,128)S(1)} all-gather(f32[1,4,2016]{2,1,0:T(4,128)S(1)} %bitcast.43), channel_id=1, replica_groups=mesh['frame'=4,'crop'=4,'dp'=2] {'crop','dp'}, dimensions={0}, use_global_device_ids=true | all-gather | bytes 290304 | tf_op jit(solution)/shard_map/all_gather | solution.py:526
  158.7 1.1 fusion.13
  159.8 1.1 fusion.11
  160.9 12.1 %reduce-scatter.3.cloned.1.call-done = f32[176,528]{1,0:T(8,128)} async-done(((f32[1408,528]{1,0:T(8,128)}), f32[176,528]{1,0:T(8,128)}) %reduce-scatter.3.cloned.1.call-update) | async-done | bytes 371728 | tf_op jit(solution)/shard_map/reduce_scatter | solution.py:515
  173.0 45.4 %reduce-scatter.5.cloned.1.call-done = f32[176,528]{1,0:T(8,128)} async-done(((f32[1408,528]{1,0:T(8,128)}), f32[176,528]{1,0:T(8,128)}) %reduce-scatter.5.cloned.1.call-update) | async-done | bytes 371728 | tf_op jit(solution)/shard_map/reduce_scatter | solution.py:515
  218.3 2.2 pad_maximum_fusion
  (42 shorter events, 3.1 us)
Async XLA Ops:
  7.2 89.1 %copy-start = (bf16[256,2048]{1,0:T(8,128)(2,1)S(1)}, bf16[256,2048]{1,0:T(8,128)(2,1)}, u32[]{:S(2)}) copy-start(bf16[256,2048]{1,0:T(8,128)(2,1)} %param.18) | copy-start | bytes 3145732
  7.2 165.8 %reduce-scatter.3.cloned.1.call-start = ((), (), s32[]{:S(2)}) async-start(), calls=%async_computation.2 | async-start | bytes 4055040 | tf_op jit(solution)/shard_map/reduce_scatter | solution.py:515
  60.6 15.4 %copy-start.1 = (bf16[352,1408]{1,0:T(8,128)(2,1)S(1)}, bf16[352,1408]{1,0:T(8,128)(2,1)}, u32[]{:S(2)}) copy-start(bf16[352,1408]{1,0:T(8,128)(2,1)} %param.16) | copy-start | bytes 2973700
  74.6 18.2 %copy-start.3 = (f32[16,1,1408]{2,1,0:T(1,128)S(1)}, f32[16,1,1408]{2,1,0:T(1,128)}, u32[]{:S(2)}) copy-start(f32[16,1,1408]{2,1,0:T(1,128)} %get-tuple-element.14) | copy-start | bytes 270340
  74.6 18.4 %copy-start.2 = (bf16[1408,256]{1,0:T(8,128)(2,1)S(1)}, bf16[1408,256]{1,0:T(8,128)(2,1)}, u32[]{:S(2)}) copy-start(bf16[1408,256]{1,0:T(8,128)(2,1)} %param.17) | copy-start | bytes 2162692
  75.8 21.0 %copy-start.4 = (f32[2048]{0:T(1024)S(1)}, f32[2048]{0:T(1024)}, u32[]{:S(2)}) copy-start(f32[2048]{0:T(1024)} %param.19) | copy-start | bytes 24580
  126.7 91.7 %reduce-scatter.5.cloned.1.call-start = ((), (), s32[]{:S(2)}) async-start(), calls=%async_computation.3 | async-start | bytes 4055040 | tf_op jit(solution)/shard_map/reduce_scatter | solution.py:515
Sparse Core Ops, SparseCore 0:
  126.8 46.1 reduce-scatter.2
  175.4 42.8 reduce-scatter.4
